TPU v7x, 256 devices: a whole 4x4x8 slice. The times are simulated.
256 devices in a mesh: dp: 32 (over z, x), mp: 8 (over y, core).
Axes of the slice: x: 4, y: 4, z: 8, core: 2. Of those that a mesh axis runs over, the one named last changes fastest.
Arguments:
- qkv_rows: bfloat16 [16384, 3, 3072], P('dp', None, 'mp'), may hold values from -8 to 8
- out_weight: bfloat16 [3072, 6144], P('mp'), may hold values from -0.109375 to 0.109375
- out_grad: bfloat16 [12288, 6144], P('dp', 'mp'), may hold values from -6 to 6
- image_len: int32 [256], replicated, may hold values from 0 to 256, as said below
- dest_rank: int32 [256], replicated, may hold values from 0 to 31, as said below
- dest_offset: int32 [256], replicated, may hold values from 0 to 320, as said below
Outputs:
- mixed: bfloat16 [12288, 6144], P('dp', 'mp')
- qkv_grad: bfloat16 [16384, 3, 3072], P('dp', None, 'mp')
- weight_grad: bfloat16 [3072, 6144], P('mp', 'dp')
Inputs may be any that keep to these rules, and one draw needn't show every extreme that they name: `image_len`: patch counts are multiples of 64; 0 marks an empty slot, whose rank is its own and whose offset is 0. Every rank holds 5, 6, 7 or 8 times 64 rows from row 0 and at least one image has 256 patches. `dest_rank`: only slots 5, 6 and 7 move, each with 64 patches: slot 6 of rank r goes to rank (r + 1) mod 32, slot 7 to rank (r - 1) mod 32, slot 5 to rank (r + 32 / 2) mod 32, all at offset 5 * 64; a rank receives at most one image; an image that stays keeps its rows, which lie below 384; after the moves every rank holds exactly 384 rows. `dest_offset`: multiples of 64; images of one rank after the moves don't share rows.
All inputs are finite; a program needn't handle non-finite values.
Results may differ from a plain program's by a relative error of at most 0.025.
Values may be sent and summed in bfloat16 or wider, within the bound.
A program may use at most 128 MiB of HBM per device.

v0:
```python
import jax
import jax.numpy as jnp
from jax import lax
from jax.sharding import PartitionSpec as P

HEAD = 128
UNIT = 64
SLOTS = 8


def attend(qkv_block, seg_ids):
    row_count = qkv_block.shape[0]
    head_count = qkv_block.shape[2] // HEAD
    queries = qkv_block[:, 0].reshape(row_count, head_count, HEAD)
    keys_part = qkv_block[:, 1].reshape(row_count, head_count, HEAD)
    values_part = qkv_block[:, 2].reshape(row_count, head_count, HEAD)
    scores = jnp.einsum(
        "qhd,khd->hqk", queries, keys_part, preferred_element_type=jnp.float32
    ) * HEAD ** (-0.5)
    allowed = (seg_ids[:, None] == seg_ids[None, :]) & (seg_ids[:, None] >= 0) | jnp.eye(
        row_count, dtype=bool
    )
    scores = jnp.where(allowed[None], scores, -1e30)
    row_max = jnp.max(scores, axis=-1, keepdims=True)
    weights = jnp.exp(scores - row_max)
    probs = weights / jnp.sum(weights, axis=-1, keepdims=True)
    probs_b = probs.astype(jnp.bfloat16)
    output = jnp.einsum("hqk,khd->qhd", probs_b, values_part, preferred_element_type=jnp.float32)
    return (output.reshape(row_count, head_count * HEAD).astype(jnp.bfloat16), probs, probs_b)


def attend_back(qkv_block, probs, probs_b, grad_block):
    row_count = qkv_block.shape[0]
    head_count = qkv_block.shape[2] // HEAD
    queries = qkv_block[:, 0].reshape(row_count, head_count, HEAD)
    keys_part = qkv_block[:, 1].reshape(row_count, head_count, HEAD)
    values_part = qkv_block[:, 2].reshape(row_count, head_count, HEAD)
    grads = grad_block.reshape(row_count, head_count, HEAD)
    dprob = jnp.einsum("qhd,khd->hqk", grads, values_part, preferred_element_type=jnp.float32)
    dscore = probs * (dprob - jnp.sum(probs * dprob, axis=-1, keepdims=True)) * HEAD ** (-0.5)
    dscore_b = dscore.astype(jnp.bfloat16)
    grad_q = jnp.einsum("hqk,khd->qhd", dscore_b, keys_part, preferred_element_type=jnp.float32)
    grad_k = jnp.einsum("hqk,qhd->khd", dscore_b, queries, preferred_element_type=jnp.float32)
    grad_v = jnp.einsum("hqk,qhd->khd", probs_b, grads, preferred_element_type=jnp.float32)
    stacked = jnp.stack([grad_q, grad_k, grad_v], axis=1)
    return stacked.reshape(row_count, 3, head_count * HEAD).astype(jnp.bfloat16)


def pick_rows(source, index, valid):
    taken = jnp.take(source, jnp.clip(index.reshape(-1), 0, source.shape[0] - 1), axis=0)
    taken = taken.reshape(index.shape + source.shape[1:])
    keep = valid.reshape(valid.shape + (1,) * (taken.ndim - valid.ndim))
    return jnp.where(keep, taken, jnp.zeros_like(taken))


def routing(image_len, dest_rank, dest_offset, rank_count, rank_here, home_rows, work_rows):
    image_lens = image_len.reshape(rank_count, SLOTS)
    dest_table = dest_rank.reshape(rank_count, SLOTS)
    offset_table = dest_offset.reshape(rank_count, SLOTS)
    start_table = jnp.cumsum(image_lens, axis=1) - image_lens
    rank_ids = jnp.arange(rank_count, dtype=jnp.int32)
    moved_table = (dest_table != rank_ids[:, None]) & (image_lens > 0)
    own_lens = lax.dynamic_index_in_dim(image_lens, rank_here, 0, keepdims=False)
    own_dests = lax.dynamic_index_in_dim(dest_table, rank_here, 0, keepdims=False)
    own_starts = lax.dynamic_index_in_dim(start_table, rank_here, 0, keepdims=False)
    own_moved = lax.dynamic_index_in_dim(moved_table, rank_here, 0, keepdims=False)
    out_hit = own_moved[None, :] & (own_dests[None, :] == rank_ids[:, None])
    out_start = jnp.sum(jnp.where(out_hit, own_starts[None, :], 0), axis=1)
    out_has = jnp.any(out_hit, axis=1)
    in_hit = moved_table & (dest_table == rank_here)
    in_start = jnp.sum(jnp.where(in_hit, offset_table, 0), axis=1)
    in_has = jnp.any(in_hit, axis=1)
    home_pos = jnp.arange(home_rows, dtype=jnp.int32)
    slot_ids = jnp.arange(SLOTS, dtype=jnp.int32)
    inside = (home_pos[:, None] >= own_starts[None, :]) & (
        home_pos[:, None] < (own_starts + own_lens)[None, :]
    )
    home_seg = jnp.where(
        jnp.any(inside, axis=1), jnp.sum(jnp.where(inside, slot_ids[None, :], 0), axis=1), -1
    )
    home_stay = jnp.any(inside & ~own_moved[None, :], axis=1)
    work_pos = jnp.arange(work_rows, dtype=jnp.int32)
    stay_work = home_stay[:work_rows]
    incoming = (
        in_has[None, :]
        & (work_pos[:, None] >= in_start[None, :])
        & (work_pos[:, None] < in_start[None, :] + UNIT)
    )
    incoming_any = jnp.any(incoming, axis=1)
    source_rank = jnp.sum(jnp.where(incoming, rank_ids[None, :], 0), axis=1)
    source_row = jnp.sum(
        jnp.where(incoming, rank_ids[None, :] * UNIT + work_pos[:, None] - in_start[None, :], 0),
        axis=1,
    )
    work_index = jnp.where(stay_work, work_pos, home_rows + source_row)
    work_valid = stay_work | incoming_any
    work_seg = jnp.where(
        stay_work, home_seg[:work_rows], jnp.where(incoming_any, SLOTS + source_rank, -1)
    )
    outgoing = (
        out_has[None, :]
        & (home_pos[:, None] >= out_start[None, :])
        & (home_pos[:, None] < out_start[None, :] + UNIT)
    )
    return_row = jnp.sum(
        jnp.where(outgoing, rank_ids[None, :] * UNIT + home_pos[:, None] - out_start[None, :], 0),
        axis=1,
    )
    home_index = jnp.where(home_stay, jnp.minimum(home_pos, work_rows - 1), work_rows + return_row)
    home_valid = home_stay | jnp.any(outgoing, axis=1)
    piece_rows = jnp.arange(UNIT, dtype=jnp.int32)
    send_home = out_start[:, None] + piece_rows[None, :]
    send_home_ok = jnp.broadcast_to(out_has[:, None], send_home.shape)
    send_work = in_start[:, None] + piece_rows[None, :]
    send_work_ok = jnp.broadcast_to(in_has[:, None], send_work.shape)
    prev_one = jnp.remainder(rank_here - 1, rank_count)
    next_one = jnp.remainder(rank_here + 1, rank_count)
    across = jnp.remainder(rank_here + rank_count // 2, rank_count)
    part_row = source_row - source_rank * UNIT
    in_place = jnp.where(
        source_rank == prev_one, 0, jnp.where(source_rank == next_one, UNIT, 2 * UNIT)
    )
    near_work_index = jnp.where(stay_work, work_pos, home_rows + in_place + part_row)
    out_dest = jnp.sum(jnp.where(outgoing, rank_ids[None, :], 0), axis=1)
    home_part = return_row - out_dest * UNIT
    out_place = jnp.where(out_dest == next_one, 0, jnp.where(out_dest == prev_one, UNIT, 2 * UNIT))
    near_home_index = jnp.where(
        home_stay, jnp.minimum(home_pos, work_rows - 1), work_rows + out_place + home_part
    )
    lead_rows = jnp.stack(
        [own_starts[6] + piece_rows, own_starts[7] + piece_rows, own_starts[5] + piece_rows], axis=0
    )
    lead_flags = jnp.stack([own_moved[6], own_moved[7], own_moved[5]], axis=0)
    lead_ok = jnp.broadcast_to(lead_flags[:, None], lead_rows.shape)
    start_prev = lax.dynamic_index_in_dim(in_start, prev_one, 0, keepdims=False)
    start_next = lax.dynamic_index_in_dim(in_start, next_one, 0, keepdims=False)
    start_across = lax.dynamic_index_in_dim(in_start, across, 0, keepdims=False)
    has_prev = lax.dynamic_index_in_dim(in_has, prev_one, 0, keepdims=False)
    has_next = lax.dynamic_index_in_dim(in_has, next_one, 0, keepdims=False)
    has_across = lax.dynamic_index_in_dim(in_has, across, 0, keepdims=False)
    back_rows = jnp.stack(
        [start_prev + piece_rows, start_next + piece_rows, start_across + piece_rows], axis=0
    )
    back_flags = jnp.stack([has_prev, has_next, has_across], axis=0)
    back_ok = jnp.broadcast_to(back_flags[:, None], back_rows.shape)
    return (
        work_index,
        work_valid,
        work_seg,
        home_index,
        home_valid,
        home_seg,
        send_home,
        send_home_ok,
        send_work,
        send_work_ok,
        near_work_index,
        near_home_index,
        lead_rows,
        lead_ok,
        back_rows,
        back_ok,
    )


def body(qkv_rows, out_weight, out_grad, image_len, dest_rank, dest_offset):
    rank_count = lax.axis_size("dp")
    rank_here = lax.axis_index("dp")
    home_rows = qkv_rows.shape[0]
    work_rows = out_grad.shape[0]
    plan = routing(image_len, dest_rank, dest_offset, rank_count, rank_here, home_rows, work_rows)
    work_index, work_valid, work_seg, home_index, home_valid, home_seg = (
        plan[0],
        plan[1],
        plan[2],
        plan[3],
        plan[4],
        plan[5],
    )
    send_home, send_home_ok, send_work, send_work_ok = (plan[6], plan[7], plan[8], plan[9])
    outbound = pick_rows(qkv_rows, send_home, send_home_ok)
    arrived = lax.all_to_all(outbound, "dp", split_axis=0, concat_axis=0, tiled=True)
    row_pool = jnp.concatenate([qkv_rows, arrived.reshape((-1,) + qkv_rows.shape[1:])], axis=0)
    work_qkv = pick_rows(row_pool, work_index, work_valid)
    att_work, probs, probs_b = attend(work_qkv, work_seg)
    partial_value = jnp.dot(att_work, out_weight, preferred_element_type=jnp.float32)
    mixed = lax.psum_scatter(
        partial_value.astype(jnp.bfloat16), "mp", scatter_dimension=1, tiled=True
    )
    grad_full = lax.all_gather(out_grad, "mp", axis=1, tiled=True)
    att_grad_work = lax.dot_general(
        grad_full, out_weight, (((1,), (1,)), ((), ())), preferred_element_type=jnp.float32
    ).astype(jnp.bfloat16)
    weight_term = lax.dot_general(
        att_work, grad_full, (((0,), (0,)), ((), ())), preferred_element_type=jnp.float32
    )
    weight_grad = lax.psum_scatter(
        weight_term.astype(jnp.bfloat16), "dp", scatter_dimension=1, tiled=True
    )
    grads_work = attend_back(work_qkv, probs, probs_b, att_grad_work)
    returning = pick_rows(grads_work, send_work, send_work_ok)
    returned = lax.all_to_all(returning, "dp", split_axis=0, concat_axis=0, tiled=True)
    grad_pool = jnp.concatenate(
        [grads_work, returned.reshape((-1,) + grads_work.shape[1:])], axis=0
    )
    qkv_grad = pick_rows(grad_pool, home_index, home_valid)
    return (mixed, qkv_grad, weight_grad)


def solution(mesh):
    return jax.shard_map(
        body,
        mesh=mesh,
        in_specs=(P("dp", None, "mp"), P("mp", None), P("dp", "mp"), P(), P(), P()),
        out_specs=(P("dp", "mp"), P("dp", None, "mp"), P("mp", "dp")),
        check_vma=False,
    )
```

profile of v0, /device:TPU:4, one launch (start us, length us, event | category | flops | bytes accessed | tf_op | source)
XLA Modules:
  0.0 538.8 jit_solution(16394939666204980415)
XLA Ops:
  7.2 0.8 reshape.259
  7.9 0.8 reshape.260
  8.7 0.2 reduce_window_sum.11
  8.9 0.1 fusion.50
  9.6 47.6 %gather_fusion = bf16[2048,3,384]{2,0,1:T(8,128)(2,1)} fusion(bf16[512,3,384]{2,0,1:T(8,128)(2,1)} %param.6, s32[2048]{0:T(1024)S(1)} %broadcast_clamp_fusion.1), kind=kCustom, calls=%fused_computation | custom fusion | bytes 9445376 | tf_op jit(solution)/shard_map/jit(_take)/gather | solution.py:50
  57.2 2.9 select_select_fusion.1
  60.0 2.7 copy.59
  62.8 11.8 %all-to-all-start = ((bf16[32,64,3,384]{3,1,2,0:T(8,128)(2,1)}), bf16[32,64,3,384]{3,1,2,0:T(8,128)(2,1)}, u32[]{:S(2)}, u32[]{:S(2)}) async-start(bf16[32,64,3,384]{3,1,2,0:T(8,128)(2,1)} %copy.59), calls=%async_computation | async-start | bytes 9437184 | tf_op jit(solution)/shard_map/all_to_all | solution.py:182
  74.6 0.7 all-gather.2.cloned.1.call-update
  75.4 1.0 copy.61
  77.1 0.2 copy-done.10
  77.4 0.2 fusion.23
  77.6 100.8 %all-to-all-done = bf16[32,64,3,384]{3,1,2,0:T(8,128)(2,1)} async-done(((bf16[32,64,3,384]{3,1,2,0:T(8,128)(2,1)}), bf16[32,64,3,384]{3,1,2,0:T(8,128)(2,1)}, u32[]{:S(2)}, u32[]{:S(2)}) %all-to-all-start) | async-done | bytes 4718624 | tf_op jit(solution)/shard_map/all_to_all | solution.py:182
  178.3 6.7 %copy.60 = bf16[32,64,3,384]{3,2,1,0:T(4,128)(2,1)S(1)} copy(bf16[32,64,3,384]{3,1,2,0:T(8,128)(2,1)} %all-to-all-done) | data formatting | bytes 9437184 | tf_op jit(solution)/shard_map/all_to_all | solution.py:182
  185.1 18.2 %pad_maximum_fusion = bf16[2560,3,384]{2,1,0:T(4,128)(2,1)} fusion(bf16[2048,3,384]{2,1,0:T(4,128)(2,1)S(1)} %bitcast.50, bf16[512,3,384]{2,1,0:T(4,128)(2,1)S(1)} %copy.61), kind=kLoop, calls=%fused_computation.8 | loop fusion | flops 2949120 | bytes 11796480 | tf_op jit(solution)/shard_map/concatenate | solution.py:183
  203.3 5.2 gather_fusion.1
  208.5 1.9 select_select_fusion.3
  210.4 1.2 fusion.52
  211.7 0.9 copy.64
  212.6 0.9 copy.63
  213.4 1.0 copy.62
  214.5 2.0 fusion.54
  216.5 1.8 convolution_convert_fusion.4
  218.3 7.6 %convolution_convert_fusion = bf16[384,6144]{0,1:T(8,128)(2,1)} fusion(bf16[384,384]{0,1:T(8,128)(2,1)S(1)} %bitcast.52, bf16[384,6144]{1,0:T(8,128)(2,1)} %all-gather.2.cloned.1.call-done), kind=kOutput, calls=%fused_computation.6 | convolution fusion | flops 1814298624 | bytes 9732096 | tf_op jit(solution)/shard_map/dot_general | solution.py:194
  226.3 6.5 %convolution_convert_fusion.2 = bf16[384,384]{0,1:T(8,128)(2,1)S(1)} fusion(bf16[384,6144]{1,0:T(8,128)(2,1)} %all-gather.2.cloned.1.call-done, bf16[384,6144]{1,0:T(8,128)(2,1)} %param.7), kind=kOutput, calls=%fused_computation.21 | convolution fusion | flops 1812086784 | bytes 9732096 | tf_op jit(solution)/shard_map/dot_general | solution.py:191
  232.8 0.4 convolution_convert_fusion.3
  233.3 0.7 copy.75
  233.9 0.4 fusion.55
  234.4 3.3 fusion.12
  237.8 0.7 copy.73
  238.5 3.9 fusion.15
  242.3 0.7 copy.74
  243.0 2.1 pad_maximum_fusion.2
  245.1 19.4 %gather_fusion.2 = bf16[2048,3,384]{2,1,0:T(4,128)(2,1)} fusion(bf16[384,3,384]{2,1,0:T(4,128)(2,1)S(1)} %pad_maximum_fusion.2, s32[2048]{0:T(1024)S(1)} %broadcast_clamp_fusion), kind=kCustom, calls=%fused_computation.2 | custom fusion | bytes 9445376 | tf_op jit(solution)/shard_map/jit(_take)/gather | solution.py:50
  264.5 3.5 copy.76
  268.0 1.2 select_select_fusion
  269.2 2.6 copy.77
  271.8 10.5 %all-to-all-start.1 = ((bf16[32,64,3,384]{3,1,2,0:T(8,128)(2,1)}), bf16[32,64,3,384]{3,1,2,0:T(8,128)(2,1)}, u32[]{:S(2)}, u32[]{:S(2)}) async-start(bf16[32,64,3,384]{3,1,2,0:T(8,128)(2,1)} %copy.77), calls=%async_computation.2 | async-start | bytes 9437184 | tf_op jit(solution)/shard_map/all_to_all | solution.py:202
  282.4 7.2 %convolution_convert_fusion.1 = bf16[384,6144]{1,0:T(8,128)(2,1)} fusion(bf16[384,384]{0,1:T(8,128)(2,1)S(1)} %bitcast.53, bf16[384,6144]{1,0:T(8,128)(2,1)} %param.7), kind=kOutput, calls=%fused_computation.7 | convolution fusion | flops 1814298624 | bytes 9732096 | tf_op jit(solution)/shard_map/dot_general | solution.py:186
  289.6 0.6 copy-done.13
  290.5 107.6 %all-to-all-done.1 = bf16[32,64,3,384]{3,1,2,0:T(8,128)(2,1)} async-done(((bf16[32,64,3,384]{3,1,2,0:T(8,128)(2,1)}), bf16[32,64,3,384]{3,1,2,0:T(8,128)(2,1)}, u32[]{:S(2)}, u32[]{:S(2)}) %all-to-all-start.1) | async-done | bytes 4718624 | tf_op jit(solution)/shard_map/all_to_all | solution.py:202
  398.1 6.8 %copy.78 = bf16[32,64,3,384]{3,2,1,0:T(4,128)(2,1)S(1)} copy(bf16[32,64,3,384]{3,1,2,0:T(8,128)(2,1)} %all-to-all-done.1) | data formatting | bytes 9437184 | tf_op jit(solution)/shard_map/all_to_all | solution.py:202
  404.8 35.9 %pad_maximum_fusion.1 = bf16[2432,3,384]{2,1,0:T(4,128)(2,1)} fusion(bf16[2048,3,384]{2,1,0:T(4,128)(2,1)S(1)} %bitcast.49, bf16[384,1,384]{2,1,0:T(2,128)(2,1)S(1)} %copy.75, bf16[384,1,384]{2,1,0:T(2,128)(2,1)S(1)} %copy.74, bf16[384,1,384]{2,1,0:T(2,128)(2,1)S(1)} %copy.73), kind=kLoop, calls=%fused_computation.9 | loop fusion | flops 22413312 | bytes 11206656 | tf_op jit(solution)/shard_map/concatenate | solution.py:203
  440.7 5.5 %gather_fusion.3 = bf16[512,3,384]{2,1,0:T(4,128)(2,1)S(1)} fusion(bf16[2432,3,384]{2,1,0:T(4,128)(2,1)} %pad_maximum_fusion.1, s32[1024]{0:T(1024)S(1)} %pad_clamp_fusion), kind=kCustom, calls=%fused_computation.3 | custom fusion | bytes 2361344 | tf_op jit(solution)/shard_map/jit(_take)/gather | solution.py:50
  446.3 3.1 select_select_fusion.2
  449.4 1.2 copy.79
  450.6 37.4 %reduce-scatter.5.cloned.1.call-done = bf16[384,192]{0,1:T(8,128)(2,1)} async-done(((bf16[384,6144]{0,1:T(8,128)(2,1)}), bf16[384,192]{0,1:T(8,128)(2,1)}) %reduce-scatter.5.cloned.1.call-update) | async-done | bytes 147472 | tf_op jit(solution)/shard_map/reduce_scatter | solution.py:197
  488.0 43.9 %reduce-scatter.3.cloned.1.call-done = bf16[384,768]{1,0:T(8,128)(2,1)} async-done(((bf16[384,6144]{1,0:T(8,128)(2,1)}), bf16[384,768]{1,0:T(8,128)(2,1)}) %reduce-scatter.3.cloned.1.call-update) | async-done | bytes 589840 | tf_op jit(solution)/shard_map/reduce_scatter | solution.py:187
  (75 shorter events, 1.9 us)
Async XLA Ops:
  9.0 67.9 %copy-start.8 = (pred[32]{0:T(512)(128)(4,1)}, pred[32]{0:T(512)(128)(4,1)S(1)}, u32[]{:S(2)}) copy-start(pred[32]{0:T(512)(128)(4,1)S(1)} %get-tuple-element.20) | copy-start | bytes 100
  9.2 48.0 %copy-start.12 = (pred[32]{0:T(512)(128)(4,1)}, pred[32]{0:T(512)(128)(4,1)S(1)}, u32[]{:S(2)}) copy-start(pred[32]{0:T(512)(128)(4,1)S(1)} %fusion.36) | copy-start | bytes 100
  62.8 12.6 %copy-start = (bf16[512,3,384]{2,0,1:T(8,128)(2,1)S(1)}, bf16[512,3,384]{2,0,1:T(8,128)(2,1)}, u32[]{:S(2)}) copy-start(bf16[512,3,384]{2,0,1:T(8,128)(2,1)} %param.6) | copy-start | bytes 3538948
  62.8 115.5 %all-to-all-start = ((bf16[32,64,3,384]{3,1,2,0:T(8,128)(2,1)}), bf16[32,64,3,384]{3,1,2,0:T(8,128)(2,1)}, u32[]{:S(2)}, u32[]{:S(2)}) async-start(bf16[32,64,3,384]{3,1,2,0:T(8,128)(2,1)} %copy.59), calls=%async_computation | async-start | bytes 9437184 | tf_op jit(solution)/shard_map/all_to_all | solution.py:182
  74.6 1.8 copy-start.16
  74.6 143.8 %all-gather.2.cloned.1.call-start = ((), (), s32[]{:S(2)}) async-start(), calls=%async_computation.5 | async-start | bytes 5308416 | tf_op jit(solution)/shard_map/all_gather | solution.py:190
  75.3 412.7 %reduce-scatter.5.cloned.1.call-start = ((), (), s32[]{:S(2)}) async-start(), calls=%async_computation.6 | async-start | bytes 4866048 | tf_op jit(solution)/shard_map/reduce_scatter | solution.py:197
  76.8 0.5 copy-start.10
  76.8 0.6 copy-start.14
  212.5 3.9 copy-start.6
  213.4 3.0 copy-start.4
  216.5 16.3 %copy-start.18 = (f32[3,384]{1,0:T(4,128)}, f32[3,384]{1,0:T(4,128)S(1)}, u32[]{:S(2)}) copy-start(f32[3,384]{1,0:T(4,128)S(1)} %get-tuple-element.35) | copy-start | bytes 13828
  218.3 7.7 %copy-start.2 = (bf16[3,128,384]{2,1,0:T(8,128)(2,1)}, bf16[3,128,384]{2,1,0:T(8,128)(2,1)S(1)}, u32[]{:S(2)}) copy-start(bf16[3,128,384]{2,1,0:T(8,128)(2,1)S(1)} %convolution_convert_fusion.4) | copy-start | bytes 884740
  226.3 6.5 %copy-start.17 = (f32[3,384,384]{1,2,0:T(8,128)S(1)}, f32[3,384,384]{1,2,0:T(8,128)}, u32[]{:S(2)}) copy-start(f32[3,384,384]{1,2,0:T(8,128)} %get-tuple-element.36) | copy-start | bytes 5308420
  233.2 1.1 copy-start.7
  234.4 3.4 copy-start.1
  234.4 4.0 copy-start.5
  234.4 4.0 copy-start.19
  264.5 3.5 copy-start.9
  271.8 10.6 %copy-start.3 = (bf16[3,128,384]{2,1,0:T(8,128)(2,1)S(1)}, bf16[3,128,384]{2,1,0:T(8,128)(2,1)}, u32[]{:S(2)}) copy-start(bf16[3,128,384]{2,1,0:T(8,128)(2,1)} %copy-done.2) | copy-start | bytes 884740
  271.8 126.3 %all-to-all-start.1 = ((bf16[32,64,3,384]{3,1,2,0:T(8,128)(2,1)}), bf16[32,64,3,384]{3,1,2,0:T(8,128)(2,1)}, u32[]{:S(2)}, u32[]{:S(2)}) async-start(bf16[32,64,3,384]{3,1,2,0:T(8,128)(2,1)} %copy.77), calls=%async_computation.2 | async-start | bytes 9437184 | tf_op jit(solution)/shard_map/all_to_all | solution.py:202
  282.3 249.5 %reduce-scatter.3.cloned.1.call-start = ((), (), s32[]{:S(2)}) async-start(), calls=%async_computation.4 | async-start | bytes 5308416 | tf_op jit(solution)/shard_map/reduce_scatter | solution.py:187
  289.6 0.7 copy-start.13
  289.6 0.7 copy-start.15
  289.6 0.8 copy-start.11
Sparse Core Ops, SparseCore 0:
  77.2 37.9 all-gather.1
  226.1 261.8 reduce-scatter.4
  491.1 40.6 reduce-scatter.2
where the time goes:
time: 547 us; the launch traced here: 539 us
  waiting for transfers between devices  290 us (53%)
  local copies, waits for them, and re-layouts  111 us (20%)
  other arithmetic  67.1 us (12%)
  matrix products  33.2 us (6%)
  starting transfers between devices  22.4 us (4%)
  between operations  14.7 us (3%)
    all_to_all x1, waiting for transfers between devices, body(): lax.all_to_all(returning, 'dp', split_axis=0, concat_axis=0, tiled=True)  108 us
    all_to_all x1, waiting for transfers between devices, body(): lax.all_to_all(outbound, 'dp', split_axis=0, concat_axis=0, tiled=True)  101 us
    gather x5, local copies, waits for them, and re-layouts, pick_rows(): jnp.take(source, jnp.clip(index.reshape(-1), 0, source.shape[0] - 1), axi...  81.2 us
    reduce_scatter x1, waiting for transfers between devices, body(): lax.psum_scatter(partial_value.astype(jnp.bfloat16), 'mp', scatter_dimens...  43.9 us
    reduce_scatter x1, waiting for transfers between devices, body(): lax.psum_scatter(weight_term.astype(jnp.bfloat16), 'dp', scatter_dimensio...  37.4 us
    concatenate x1, other arithmetic, body(): jnp.concatenate([grads_work, returned.reshape((-1,) + grads_work.shape[1:...  35.9 us
    concatenate x1, other arithmetic, body(): jnp.concatenate([qkv_rows, arrived.reshape((-1,) + qkv_rows.shape[1:])],...  18.2 us
    all_to_all x1, starting transfers between devices, body(): lax.all_to_all(outbound, 'dp', split_axis=0, concat_axis=0, tiled=True)  11.8 us
  transfers between devices with their start and end apart: 5, of which 4 were waited for; matrix products, arithmetic and copies ran while one was open for 27% of the time, Pallas kernels for 0%

commit v1 on v0

v1 whole, which is shorter than its diff:
```python
import functools

import jax
import jax.numpy as jnp
from jax import lax
from jax.experimental import pallas as pl
from jax.experimental.pallas import tpu as pltpu
from jax.sharding import PartitionSpec as P

HEAD = 128
UNIT = 64
SLOTS = 8
NZ, NX, NY = 8, 4, 4
NDP = NZ * NX
HOME = 512
CAP = 384
HEADS = 3
INN = HEADS * HEAD
COLS = 768
DOWN = 1 / HEAD ** 0.5
MESH = pl.DeviceIdType.MESH
F32 = jnp.float32
BF = jnp.bfloat16
HALF = CAP // 2
RX = 256
RZ = 128
PX = RX // NX
PZ = RZ // NX
WINDOWS = ((0, 384), (0, 512), (0, 512), (128, 512))


def add(a, b):
    return (a.astype(F32) + b.astype(F32)).astype(BF)


def nt(a, b):
    return lax.dot_general(a, b, (((1,), (1,)), ((), ())), preferred_element_type=F32)


def nn(a, b):
    return jnp.dot(a, b, preferred_element_type=F32)


def kernel(len_ref, dest_ref, qkv_hbm, w_hbm, g_hbm, mixed_ref, dqkv_ref, wg_ref,
           qkv, w, gb, bias, probs, att_home, att_send, att_recv, att, att_t, acc, agw, back_recv,
           ghome, dk_t, dv_t, wt1, wt2, psend, precv, rbuf, yrp, yrm, xlp, xlm, xrp, xrm, xr,
           z1p, z1m, z2p, z2m, zr2, x2p, x2m, wfin, wrecv, ss, rs, ls):
    dp, mp = lax.axis_index("dp"), lax.axis_index("mp")
    z, x = lax.div(dp, NX), lax.rem(dp, NX)
    y, c = lax.div(mp, 2), lax.rem(mp, 2)

    def at_y(d):
        return lax.rem(y + d + NY, NY)

    def at_x(d):
        return lax.rem(x + d + NX, NX)

    def at_z(d):
        return lax.rem(z + d + NZ, NZ)

    def at_dp(d):
        return lax.rem(dp + d + NDP, NDP)

    sib = (dp, 2 * y + 1 - c)
    yp, ym = (dp, 2 * at_y(1) + c), (dp, 2 * at_y(-1) + c)
    xp, xm, xo = (z * NX + at_x(1), mp), (z * NX + at_x(-1), mp), (z * NX + at_x(2), mp)
    zp, zm = (at_z(1) * NX + x, mp), (at_z(-1) * NX + x, mp)
    nxt, prv, acr = (at_dp(1), mp), (at_dp(-1), mp), (at_dp(NDP // 2), mp)
    partners = (sib, yp, ym, xp, xm, xo, zp, zm, nxt, prv, acr)

    in_g = pltpu.make_async_copy(g_hbm, gb.at[0], ls.at[0])
    in_qkv = pltpu.make_async_copy(qkv_hbm, qkv, ls.at[1])
    in_w = pltpu.make_async_copy(w_hbm, w, ls.at[2])
    in_g.start()
    in_qkv.start()
    in_w.start()

    barrier = pltpu.get_barrier_semaphore()
    for one in partners:
        pl.semaphore_signal(barrier, inc=1, device_id=one, device_id_type=MESH)
    pl.semaphore_wait(barrier, len(partners))

    sent = []

    def send(src, dst, to):
        i = len(sent)
        copy = pltpu.make_async_remote_copy(
            src_ref=src, dst_ref=dst, send_sem=ss.at[i], recv_sem=rs.at[i], device_id=to,
            device_id_type=MESH)
        copy.start()
        sent.append(copy)
        return copy

    top, bot = pl.ds(0, HALF), pl.ds(HALF, HALF)

    in_g.wait()
    g_yp_top = send(gb.at[0, top], gb.at[2, top], yp)
    g_ym_bot = send(gb.at[0, bot], gb.at[3, bot], ym)
    g_yp_bot = send(gb.at[0, bot], gb.at[2, bot], yp)
    g_ym_top = send(gb.at[0, top], gb.at[3, top], ym)
    g_sib = send(gb.at[0], gb.at[1], sib)

    def ends_of(rank):
        ends, total = [], jnp.int32(0)
        for s in range(SLOTS):
            total = total + len_ref[rank * SLOTS + s]
            ends.append(total)
        return ends

    ends = ends_of(dp)

    def moved(rank, slot):
        return (dest_ref[rank * SLOTS + slot] != rank) & (len_ref[rank * SLOTS + slot] > 0)

    def image_of(pos):
        out = jnp.zeros(pos.shape, jnp.int32)
        for end in ends:
            out = out + (pos >= end).astype(jnp.int32)
        return out

    rows_at = image_of(lax.broadcasted_iota(jnp.int32, (HOME, 1), 0))
    cols_at = image_of(lax.broadcasted_iota(jnp.int32, (1, HOME), 1))
    bias[...] = jnp.where(rows_at == cols_at, 0.0, -1e30).astype(F32)

    in_qkv.wait()

    def forward(h, carry):
        at = pl.multiple_of(h * HEAD, HEAD)
        for i, (lo, hi) in enumerate(WINDOWS):
            rows, keys = pl.ds(i * 128, 128), pl.ds(lo, hi - lo)
            q = qkv[rows, pl.ds(at, HEAD)]
            k = qkv[keys, pl.ds(at + INN, HEAD)]
            v = qkv[keys, pl.ds(at + 2 * INN, HEAD)]
            s = nt(q, k) * DOWN + bias[rows, keys]
            e = jnp.exp(s - jnp.max(s, axis=-1, keepdims=True))
            p = e / jnp.sum(e, axis=-1, keepdims=True)
            probs[h, rows, keys] = p
            att_home[rows, pl.ds(at, HEAD)] = nn(p.astype(BF), v).astype(BF)
        return carry

    lax.fori_loop(0, HEADS, forward, 0)

    def unit(ref, u):
        return ref[pl.ds(u * UNIT, UNIT), :].astype(F32)

    starts = [jnp.int32(0)] + ends[:-1]
    for i, slot in enumerate((6, 7, 5)):
        pick = jnp.where(starts[slot] == 5 * UNIT, unit(att_home, 5),
                         jnp.where(starts[slot] == 6 * UNIT, unit(att_home, 6), unit(att_home, 7)))
        att_send[i] = pick.astype(BF)
    moves = [send(att_send.at[i], att_recv.at[i], to) for i, to in enumerate((nxt, prv, acr))]

    g_yp_top.wait_recv()
    g_yo_top = send(gb.at[2, top], gb.at[6, top], yp)
    g_sib_4t = send(gb.at[2, top], gb.at[4, top], sib)
    g_ym_bot.wait_recv()
    g_yo_bot = send(gb.at[3, bot], gb.at[6, bot], ym)
    g_sib_5b = send(gb.at[3, bot], gb.at[5, bot], sib)

    for m in moves:
        m.wait_recv()
    from_prv, from_nxt, from_acr = moved(at_dp(-1), 6), moved(at_dp(1), 7), moved(at_dp(NDP // 2), 5)
    last = jnp.where(from_prv, att_recv[0].astype(F32),
                     jnp.where(from_nxt, att_recv[1].astype(F32),
                               jnp.where(from_acr, att_recv[2].astype(F32), unit(att_home, 5))))
    att[pl.ds(0, 5 * UNIT), :] = att_home[pl.ds(0, 5 * UNIT), :]
    att[pl.ds(5 * UNIT, UNIT), :] = last.astype(BF)
    att_t[...] = att[...].astype(F32).T.astype(BF)

    def flip_of(f):
        return c + f - 2 * c * f

    def first_group(j):
        return 2 * y + flip_of(j)

    def second_group(j):
        i = j - 2
        return 2 * at_y(2 * lax.rem(i, 2) - 1) + flip_of(lax.div(i, 2))

    def third_group(j):
        return 2 * at_y(2) + flip_of(j - 6)

    in_w.wait()
    acc[...] = jnp.zeros_like(acc)

    def cols_of(block):
        return pl.ds(pl.multiple_of(block * COLS, COLS), COLS)

    def terms(lo, hi, block_of):
        def one(j, carry):
            block = block_of(j)
            t = nn(att_t[...], gb[j]).astype(BF)
            wt1[j] = t[:RX]
            wt2[block] = t[RX:]
            return carry

        lax.fori_loop(lo, hi, one, 0)

    def grads(lo, hi, block_of):
        def one(j, carry):
            acc[...] += nt(gb[j], w[:, cols_of(block_of(j))])
            return carry

        lax.fori_loop(lo, hi, one, 0)

    def along_x(lo, half, block_of):
        far, right, left = (pl.ds(pl.multiple_of(at_x(d) * PX, PX), PX) for d in (2, 1, -1))
        mine = pl.ds(pl.multiple_of(x * PX, PX), PX)
        a, b = pl.ds(lo, half), pl.ds(lo + half, half)
        la = pl.ds(lo // 2, half)
        relay_p = send(wt1.at[a, far], xlp.at[la], xp)
        relay_m = send(wt1.at[b, far], xlm.at[la], xm)
        early_p = send(wt1.at[b, right], xrp.at[b], xp)
        early_m = send(wt1.at[a, left], xrm.at[a], xm)
        yield
        relay_p.wait_recv()
        for i in range(half):
            wt1[lo + i, right] = add(wt1[lo + i, right], xlp[lo // 2 + i])
        late_p = send(wt1.at[a, right], xrp.at[a], xp)
        relay_m.wait_recv()
        for i in range(half):
            wt1[lo + half + i, left] = add(wt1[lo + half + i, left], xlm[lo // 2 + i])
        late_m = send(wt1.at[b, left], xrm.at[b], xm)
        yield
        for copy in (early_p, early_m, late_p, late_m):
            copy.wait_recv()

        def one(j, carry):
            total = wt1[j, mine].astype(F32) + xrp[j].astype(F32) + xrm[j].astype(F32)
            xr[block_of(j)] = total.astype(BF)
            return carry

        lax.fori_loop(lo, lo + 2 * half, one, 0)
        yield

    def along_z(buf, rows, from_m, from_p, out):
        half = rows // 2
        up, down = pl.ds(0, half), pl.ds(half, half)
        a = send(buf.at[at_z(4), up], from_m.at[3, up], zp)
        b = send(buf.at[at_z(4), down], from_p.at[3, down], zm)
        yield
        for d in (3, 2, 1):
            part_a, part_b = (up, down) if d == 3 else (slice(None), slice(None))
            a.wait_recv()
            here = at_z(d)
            buf[here, part_a] = add(buf[here, part_a], from_m[d, part_a])
            a = send(buf.at[here], from_m.at[d - 1], zp)
            b.wait_recv()
            here = at_z(-d)
            buf[here, part_b] = add(buf[here, part_b], from_p[d, part_b])
            b = send(buf.at[here], from_p.at[d - 1], zm)
            yield
        a.wait_recv()
        b.wait_recv()
        out[...] = (buf[z].astype(F32) + from_m[0].astype(F32) + from_p[0].astype(F32)).astype(BF)
        yield

    def along_x_last():
        far, right, left, mine = (pl.multiple_of(at_x(d) * PZ, PZ) for d in (2, 1, -1, 0))
        half = PZ // 2
        up, down = pl.ds(0, half), pl.ds(half, half)
        a = send(zr2.at[pl.ds(far, half)], x2p.at[1, up], xp)
        b = send(zr2.at[pl.ds(pl.multiple_of(far + half, half), half)], x2m.at[1, down], xm)
        yield
        a.wait_recv()
        zr2[pl.ds(right, half)] = add(zr2[pl.ds(right, half)], x2p[1, up])
        a = send(zr2.at[pl.ds(right, PZ)], x2p.at[0], xp)
        b.wait_recv()
        low = pl.ds(pl.multiple_of(left + half, half), half)
        zr2[low] = add(zr2[low], x2m[1, down])
        b = send(zr2.at[pl.ds(left, PZ)], x2m.at[0], xm)
        yield
        a.wait_recv()
        b.wait_recv()
        total = zr2[pl.ds(mine, PZ)].astype(F32) + x2p[0].astype(F32) + x2m[0].astype(F32)
        wfin[pl.ds(PX, PZ)] = total.astype(BF)
        yield

    g_sib.wait_recv()
    terms(0, 2, first_group)
    x1 = along_x(0, 1, first_group)
    next(x1)

    turns = (2, 1, -1, 0)

    def turn(i):
        return lax.rem(y + 2 + 3 * i, NY)

    p_base = len(sent)

    def p_copy(i):
        return pltpu.make_async_remote_copy(
            src_ref=psend.at[i], dst_ref=precv.at[i], send_sem=ss.at[p_base + i],
            recv_sem=rs.at[p_base + i], device_id=sib, device_id_type=MESH)

    def for_sibling(i, carry):
        psend[i] = nn(att[...], w[:, cols_of(2 * turn(i) + 1 - c)]).astype(BF)
        p_copy(i).start()
        return carry

    lax.fori_loop(0, NY, for_sibling, 0)
    sent.extend(p_copy(i) for i in range(NY))

    def for_me(i, carry):
        rbuf[i] = nn(att[...], w[:, cols_of(2 * turn(i) + c)]).astype(BF)
        return carry

    lax.fori_loop(0, NY, for_me, 0)
    next(x1)

    def merge(i):
        sent[p_base + i].wait_recv()
        rbuf[i] = add(rbuf[i], precv[i])

    merge(0)
    r_far_p = send(rbuf.at[0, top], yrp.at[1, top], yp)
    r_far_m = send(rbuf.at[0, bot], yrm.at[1, bot], ym)
    merge(1)
    r_yp_bot = send(rbuf.at[1, bot], yrp.at[0, bot], yp)
    merge(3)
    r_ym_top = send(rbuf.at[3, top], yrm.at[0, top], ym)
    merge(2)

    grads(0, 2, first_group)

    g_yp_bot.wait_recv()
    g_sib_4b = send(gb.at[2, bot], gb.at[4, bot], sib)
    g_ym_top.wait_recv()
    g_sib_5t = send(gb.at[3, top], gb.at[5, top], sib)
    next(x1)
    for copy in (g_sib_4t, g_sib_4b, g_sib_5t, g_sib_5b):
        copy.wait_recv()
    terms(2, 6, second_group)
    x2 = along_x(2, 2, second_group)
    next(x2)
    grads(2, 6, second_group)

    g_yo_top.wait_recv()
    g_sib_7t = send(gb.at[6, top], gb.at[7, top], sib)
    g_yo_bot.wait_recv()
    g_sib_7b = send(gb.at[6, bot], gb.at[7, bot], sib)
    next(x2)
    g_sib_7t.wait_recv()
    g_sib_7b.wait_recv()
    terms(6, 8, third_group)
    x3 = along_x(6, 1, third_group)
    next(x3)
    z2 = along_z(wt2, RZ, z2p, z2m, zr2)
    next(z2)
    grads(6, 8, third_group)
    agw[...] = acc[...].astype(BF)
    tail = agw.at[pl.ds(5 * UNIT, UNIT)]
    backs = [send(tail, back_recv.at[i], to) for i, to in enumerate((prv, nxt, acr))]

    r_far_p.wait_recv()
    rbuf[1, top] = add(rbuf[1, top], yrp[1, top])
    r_yp_top = send(rbuf.at[1, top], yrp.at[0, top], yp)
    r_far_m.wait_recv()
    rbuf[3, bot] = add(rbuf[3, bot], yrm[1, bot])
    r_ym_bot = send(rbuf.at[3, bot], yrm.at[0, bot], ym)
    next(x2)

    for copy in backs:
        copy.wait_recv()
    got = from_prv | from_nxt | from_acr
    ghome[pl.ds(0, 5 * UNIT), :] = agw[pl.ds(0, 5 * UNIT), :]
    for u in (5, 6, 7):
        value = jnp.zeros((UNIT, INN), F32)
        for i, slot in enumerate((6, 7, 5)):
            hit = moved(dp, slot) & (starts[slot] == u * UNIT)
            value = jnp.where(hit, back_recv[i].astype(F32), value)
        if u == 5:
            value = jnp.where(got, value, unit(agw, 5))
        ghome[pl.ds(u * UNIT, UNIT), :] = value.astype(BF)

    def backward(h, carry):
        at = pl.multiple_of(h * HEAD, HEAD)
        q_t = qkv[:, pl.ds(at, HEAD)].astype(F32).T.astype(BF)
        g_t = ghome[:, pl.ds(at, HEAD)].astype(F32).T.astype(BF)
        dk_t[...] = jnp.zeros_like(dk_t)
        dv_t[...] = jnp.zeros_like(dv_t)
        for i, (lo, hi) in enumerate(WINDOWS):
            rows, keys = pl.ds(i * 128, 128), pl.ds(lo, hi - lo)
            k = qkv[keys, pl.ds(at + INN, HEAD)]
            v = qkv[keys, pl.ds(at + 2 * INN, HEAD)]
            p = probs[h, rows, keys]
            dp_ = nt(ghome[rows, pl.ds(at, HEAD)], v)
            mean = jnp.sum(p * dp_, axis=-1, keepdims=True)
            ds = (p * (dp_ - mean) * DOWN).astype(BF)
            dqkv_ref[rows, pl.ds(at, HEAD)] = nn(ds, k).astype(BF)
            mine = slice(i * 128, (i + 1) * 128)
            dk_t[:, keys] += nn(q_t[:, mine], ds)
            dv_t[:, keys] += nn(g_t[:, mine], p.astype(BF))
        dqkv_ref[:, pl.ds(at + INN, HEAD)] = dk_t[...].T.astype(BF)
        dqkv_ref[:, pl.ds(at + 2 * INN, HEAD)] = dv_t[...].T.astype(BF)
        return carry

    next(x3)
    next(z2)
    lax.fori_loop(0, 1, backward, 0)
    next(x3)
    z1 = along_z(xr, PX, z1p, z1m, wfin.at[pl.ds(0, PX)])
    next(z1)
    next(z2)
    lax.fori_loop(1, 2, backward, 0)
    next(z1)
    next(z2)
    lax.fori_loop(2, 3, backward, 0)
    next(z1)
    next(z2)
    xl = along_x_last()
    next(xl)
    next(z1)
    next(xl)
    next(z1)
    next(xl)

    def window(at):
        return pl.ds(pl.multiple_of(lax.div(at, 2) * 384 + lax.rem(at, 2) * 128, 128), 256)

    lasts = [send(wfin.at[:, window(at_x(d))], wrecv.at[i], to)
             for i, (d, to) in enumerate(((1, xp), (-1, xm), (2, xo)))]

    def place(of, rows):
        wg_ref[pl.ds(pl.multiple_of(of * PX, PX), PX), :] = rows[:PX]
        wg_ref[pl.ds(pl.multiple_of(RX + of * PZ, PZ), PZ), :] = rows[PX:]

    for copy in (r_yp_bot, r_yp_top, r_ym_top, r_ym_bot):
        copy.wait_recv()
    mixed_ref[...] = (rbuf[2].astype(F32) + yrp[0].astype(F32) + yrm[0].astype(F32)).astype(BF)

    place(x, wfin[:, window(x)])
    for i, d in enumerate((-1, 1, 2)):
        lasts[i].wait_recv()
        place(at_x(d), wrecv[i])
    for copy in sent:
        copy.wait_send()


def scratch():
    v = pltpu.VMEM
    return [
        v((HOME, 3 * INN), BF), v((INN, 8 * COLS), BF), v((8, CAP, COLS), BF), v((HOME, HOME), F32),
        v((HEADS, HOME, HOME), F32), v((HOME, INN), BF), v((3, UNIT, INN), BF), v((3, UNIT, INN), BF),
        v((CAP, INN), BF), v((INN, CAP), BF), v((CAP, INN), F32), v((CAP, INN), BF), v((3, UNIT, INN), BF),
        v((HOME, INN), BF), v((HEAD, HOME), F32), v((HEAD, HOME), F32),
        v((8, RX, COLS), BF), v((8, RZ, COLS), BF),
        v((4, CAP, COLS), BF), v((4, CAP, COLS), BF), v((4, CAP, COLS), BF),
        v((2, CAP, COLS), BF), v((2, CAP, COLS), BF),
        v((4, PX, COLS), BF), v((4, PX, COLS), BF), v((8, PX, COLS), BF), v((8, PX, COLS), BF),
        v((8, PX, COLS), BF),
        v((4, PX, COLS), BF), v((4, PX, COLS), BF), v((4, RZ, COLS), BF), v((4, RZ, COLS), BF),
        v((RZ, COLS), BF), v((2, PZ, COLS), BF), v((2, PZ, COLS), BF),
        v((PX + PZ, COLS), BF), v((3, PX + PZ, 256), BF),
        pltpu.SemaphoreType.DMA((96,)), pltpu.SemaphoreType.DMA((96,)), pltpu.SemaphoreType.DMA((3,)),
    ]


def body(qkv_rows, out_weight, out_grad, image_len, dest_rank, dest_offset):
    smem = pl.BlockSpec(memory_space=pltpu.SMEM)
    anywhere = pl.BlockSpec(memory_space=pl.ANY)
    vmem = pl.BlockSpec(memory_space=pltpu.VMEM)
    mixed, dqkv, wide = pl.pallas_call(
        kernel,
        out_shape=(
            jax.ShapeDtypeStruct((CAP, COLS), BF),
            jax.ShapeDtypeStruct((HOME, 3 * INN), BF),
            jax.ShapeDtypeStruct((INN, 256), BF),
        ),
        in_specs=[smem, smem, anywhere, anywhere, anywhere],
        out_specs=(vmem, vmem, vmem),
        scratch_shapes=scratch(),
        compiler_params=pltpu.CompilerParams(
            collective_id=0, has_side_effects=True, vmem_limit_bytes=60 * 2**20),
    )(image_len, dest_rank, qkv_rows.reshape(HOME, 3 * INN), out_weight, out_grad)
    odd = lax.rem(lax.axis_index("dp"), 2)
    weight_grad = lax.dynamic_slice_in_dim(wide, odd * 64, 192, axis=1)
    return mixed, dqkv.reshape(HOME, 3, INN), weight_grad


def solution(mesh):
    return jax.shard_map(
        body,
        mesh=mesh,
        in_specs=(P("dp", None, "mp"), P("mp", None), P("dp", "mp"), P(), P(), P()),
        out_specs=(P("dp", "mp"), P("dp", None, "mp"), P("mp", "dp")),
        check_vma=False,
    )
```

time: 547 us -> 93 us (0.17)
  the two profiles are of different devices: /device:TPU:4 before, /device:TPU:24 now
where the time goes in v1:
time: 93 us; the launch traced here: 92.8 us
  Pallas kernels  84.4 us (91%)
  local copies, waits for them, and re-layouts  7.7 us (8%)
    pallas_call x1, Pallas kernels, body(): pl.pallas_call(kernel, out_shape=(jax.ShapeDtypeStruct((CAP, COLS), BF),...  84.4 us
    unnamed x8, local copies, waits for them, and re-layouts  4.6 us

profile of v1, /device:TPU:24, one launch (start us, length us, event | category | flops | bytes accessed | tf_op | source)
XLA Modules:
  0.0 92.8 jit_solution(12521500692278036987)
XLA Ops:
  0.6 1.6 %copy.11 = bf16[512,3,384]{0,2,1:T(8,128)(2,1)S(1)} copy(bf16[512,3,384]{2,0,1:T(8,128)(2,1)} %param.6) | data formatting | bytes 2359296 | tf_op args[0]
  2.2 1.4 %copy.12.qkv_hbm = bf16[512,1152]{1,0:T(8,128)(2,1)} copy(bf16[512,1152]{0,1:T(8,128)(2,1)S(1)} %bitcast.3) | data formatting | bytes 2359296 | tf_op jit(solution)/shard_map/reshape | solution.py:475
  3.6 84.4 %shard_map.76 = (bf16[384,768]{1,0:T(8,128)(2,1)}, bf16[512,1152]{1,0:T(8,128)(2,1)}, bf16[384,256]{1,0:T(8,128)(2,1)}) custom-call(s32[256]{0:T(256)} %len_ref.1, s32[256]{0:T(256)} %dest_ref.1, bf16[512,1152]{1,0:T(8,128)(2,1)} %copy.12.qkv_hbm, bf16[384,6144]{1,0:T(8,128)(2,1)} %w_hbm.1, bf16[384,768]{1,0:T(8,128)(2,1)} %g_hbm.1), custom_call_target="tpu_custom_call" | custom-call | tf_op jit(solution)/shard_map/pallas_call | solution.py:463
  88.1 1.6 %copy.13 = bf16[512,1152]{0,1:T(8,128)(2,1)S(1)} copy(bf16[512,1152]{1,0:T(8,128)(2,1)} %get-tuple-element.7) | data formatting | bytes 2359296 | tf_op jit(solution)/shard_map/pallas_call | solution.py:463
  89.7 0.0 copy-start.1
  89.7 0.0 copy-start
  89.7 1.4 %copy.14 = bf16[512,3,384]{2,0,1:T(8,128)(2,1)} copy(bf16[512,3,384]{0,2,1:T(8,128)(2,1)S(1)} %bitcast.2) | data formatting | bytes 2359296
  91.1 0.0 copy-done.1
  91.1 0.1 constant_dynamic-slice_fusion
  91.2 0.8 copy.15
  92.0 0.0 copy-done
  92.0 0.8 copy.17
Async XLA Ops:
  89.7 1.4 %copy-start.1 = (bf16[384,256]{1,0:T(8,128)(2,1)S(1)}, bf16[384,256]{1,0:T(8,128)(2,1)}, u32[]{:S(2)}) copy-start(bf16[384,256]{1,0:T(8,128)(2,1)} %get-tuple-element.8) | copy-start | bytes 589828
  89.7 2.3 %copy-start = (bf16[384,768]{1,0:T(8,128)(2,1)S(1)}, bf16[384,768]{1,0:T(8,128)(2,1)}, u32[]{:S(2)}) copy-start(bf16[384,768]{1,0:T(8,128)(2,1)} %get-tuple-element.18) | copy-start | bytes 1769476

commit v2 on v1

v2 whole, which is shorter than its diff:
```python
import functools

import jax
import jax.numpy as jnp
from jax import lax
from jax.experimental import pallas as pl
from jax.experimental.pallas import tpu as pltpu
from jax.sharding import PartitionSpec as P

HEAD = 128
UNIT = 64
SLOTS = 8
NZ, NX, NY = 8, 4, 4
NDP = NZ * NX
HOME = 512
CAP = 384
HEADS = 3
INN = HEADS * HEAD
COLS = 768
DOWN = 1 / HEAD ** 0.5
MESH = pl.DeviceIdType.MESH
F32 = jnp.float32
BF = jnp.bfloat16
HALF = CAP // 2
LX = 256
LZ = INN - LX
PART = COLS // NX
ZROWS = 384
XROWS = 96
QUARTER = CAP // 4
WINDOWS = ((0, 384), (0, 512), (0, 512), (128, 512))


ORDER = (
    "P", "S", "F", "Q", "X1", "N", "T2A", "A", "T2B", "C", "M", "A", "X1", "W", "YF", "YE", "T3A", "T3B",
    "Z2", "X3", "C", "A", "G2", "Z2", "G3", "BK", "YL", "C", "X3", "Z2", "HM", "B0", "X3", "Z1", "Z2",
    "B1", "Z1", "Z2", "XL", "Z1", "B2", "XL", "Z1", "XL", "YD", "Z1",
)


def add(a, b):
    return (a.astype(F32) + b.astype(F32)).astype(BF)


def nt(a, b):
    return lax.dot_general(a, b, (((1,), (1,)), ((), ())), preferred_element_type=F32)


def nn(a, b):
    return jnp.dot(a, b, preferred_element_type=F32)


def kernel(len_ref, dest_ref, qkv_hbm, w_hbm, g_hbm, mixed_hbm, dqkv_hbm, wg_hbm,
           qkv, w, gb, bias, probs, att_home, att_send, att_recv, att, acc, agw, back_recv,
           ghome, dk_t, dv_t, wt1, wt2, psend, precv, rbuf, yrp, yrm, xlp, xlm, xrp, xrm, xr,
           z1p, z1m, z2p, z2m, zr2, x2p, x2m, mixed, dqkv, wg, ss, rs, ls):
    dp, mp = lax.axis_index("dp"), lax.axis_index("mp")
    z, x = lax.div(dp, NX), lax.rem(dp, NX)
    y, c = lax.div(mp, 2), lax.rem(mp, 2)

    def at_y(d):
        return lax.rem(y + d + NY, NY)

    def at_x(d):
        return lax.rem(x + d + NX, NX)

    def at_z(d):
        return lax.rem(z + d + NZ, NZ)

    def at_dp(d):
        return lax.rem(dp + d + NDP, NDP)

    sib = (dp, 2 * y + 1 - c)
    yp, ym = (dp, 2 * at_y(1) + c), (dp, 2 * at_y(-1) + c)
    xp, xm = (z * NX + at_x(1), mp), (z * NX + at_x(-1), mp)
    zp, zm = (at_z(1) * NX + x, mp), (at_z(-1) * NX + x, mp)
    nxt, prv, acr = (at_dp(1), mp), (at_dp(-1), mp), (at_dp(NDP // 2), mp)
    partners = (sib, yp, ym, xp, xm, zp, zm, nxt, prv, acr)

    in_g = pltpu.make_async_copy(g_hbm, gb.at[0], ls.at[0])
    in_qkv = pltpu.make_async_copy(qkv_hbm, qkv, ls.at[1])
    in_w = pltpu.make_async_copy(w_hbm, w, ls.at[2])
    out_mixed = pltpu.make_async_copy(mixed, mixed_hbm, ls.at[3])
    out_dqkv = pltpu.make_async_copy(dqkv, dqkv_hbm, ls.at[4])
    out_wg = pltpu.make_async_copy(wg, wg_hbm, ls.at[5])
    in_g.start()
    in_qkv.start()
    in_w.start()

    barrier = pltpu.get_barrier_semaphore()
    for one in partners:
        pl.semaphore_signal(barrier, inc=1, device_id=one, device_id_type=MESH)
    pl.semaphore_wait(barrier, len(partners))

    sent = []

    def send(src, dst, to):
        i = len(sent)
        copy = pltpu.make_async_remote_copy(
            src_ref=src, dst_ref=dst, send_sem=ss.at[i], recv_sem=rs.at[i], device_id=to,
            device_id_type=MESH)
        copy.start()
        sent.append(copy)
        return copy

    top, bot = pl.ds(0, HALF), pl.ds(HALF, HALF)

    in_g.wait()
    quarters = [pl.ds(i * QUARTER, QUARTER) for i in range(4)]
    first, later = {}, {}
    for i in range(2):
        first[i] = (send(gb.at[0, quarters[i]], gb.at[2, quarters[i]], yp),
                    send(gb.at[0, quarters[i + 2]], gb.at[3, quarters[i + 2]], ym))
    g_sib = send(gb.at[0], gb.at[1], sib)

    def ends_of(rank):
        ends, total = [], jnp.int32(0)
        for s in range(SLOTS):
            total = total + len_ref[rank * SLOTS + s]
            ends.append(total)
        return ends

    ends = ends_of(dp)

    def moved(rank, slot):
        return (dest_ref[rank * SLOTS + slot] != rank) & (len_ref[rank * SLOTS + slot] > 0)

    def image_of(pos):
        out = jnp.zeros(pos.shape, jnp.int32)
        for end in ends:
            out = out + (pos >= end).astype(jnp.int32)
        return out

    rows_at = image_of(lax.broadcasted_iota(jnp.int32, (HOME, 1), 0))
    cols_at = image_of(lax.broadcasted_iota(jnp.int32, (1, HOME), 1))
    bias[...] = jnp.where(rows_at == cols_at, 0.0, -1e30).astype(F32)

    in_qkv.wait()

    def forward(h, carry):
        at = pl.multiple_of(h * HEAD, HEAD)
        for i, (lo, hi) in enumerate(WINDOWS):
            rows, keys = pl.ds(i * 128, 128), pl.ds(lo, hi - lo)
            q = qkv[0, rows, pl.ds(at, HEAD)]
            k = qkv[1, keys, pl.ds(at, HEAD)]
            v = qkv[2, keys, pl.ds(at, HEAD)]
            s = nt(q, k) * DOWN + bias[rows, keys]
            e = jnp.exp(s - jnp.max(s, axis=-1, keepdims=True))
            p = e / jnp.sum(e, axis=-1, keepdims=True)
            probs[h, rows, keys] = p
            att_home[rows, pl.ds(at, HEAD)] = nn(p.astype(BF), v).astype(BF)
        return carry

    lax.fori_loop(0, HEADS, forward, 0)
    for i in range(2):
        later[i] = (send(gb.at[0, quarters[i + 2]], gb.at[2, quarters[i + 2]], yp),
                    send(gb.at[0, quarters[i]], gb.at[3, quarters[i]], ym))

    def unit(ref, u):
        return ref[pl.ds(u * UNIT, UNIT), :].astype(F32)

    starts = [jnp.int32(0)] + ends[:-1]
    for i, slot in enumerate((6, 7, 5)):
        pick = jnp.where(starts[slot] == 5 * UNIT, unit(att_home, 5),
                         jnp.where(starts[slot] == 6 * UNIT, unit(att_home, 6), unit(att_home, 7)))
        att_send[i] = pick.astype(BF)
    moves = [send(att_send.at[i], att_recv.at[i], to) for i, to in enumerate((nxt, prv, acr))]

    def flip_of(f):
        return c + f - 2 * c * f

    def first_group(j):
        return 2 * y + flip_of(j)

    def second_group(j):
        i = j - 2
        return 2 * at_y(2 * lax.rem(i, 2) - 1) + flip_of(lax.div(i, 2))

    def third_group(j):
        return 2 * at_y(2) + flip_of(j - 6)

    def cols_of(block):
        return pl.ds(pl.multiple_of(block * COLS, COLS), COLS)

    def terms(lo, hi, block_of):
        def one(j, carry):
            t = lax.dot_general(gb[j], att[...], (((0,), (0,)), ((), ())),
                                preferred_element_type=F32).astype(BF)
            wt1[j] = t[:, :LX]
            wt2[block_of(j)] = t[:, LX:]
            return carry

        lax.fori_loop(lo, hi, one, 0)

    def grads(lo, hi, block_of):
        def one(j, carry):
            acc[...] += nt(gb[j], w[:, cols_of(block_of(j))])
            return carry

        lax.fori_loop(lo, hi, one, 0)

    def along_x(lo, half, block_of):
        far, right, left = (pl.ds(pl.multiple_of(at_x(d) * PART, PART), PART) for d in (2, 1, -1))
        mine = pl.ds(pl.multiple_of(x * PART, PART), PART)
        a, b = pl.ds(lo, half), pl.ds(lo + half, half)
        la = pl.ds(lo // 2, half)
        relay_p = send(wt1.at[a, far], xlp.at[la], xp)
        relay_m = send(wt1.at[b, far], xlm.at[la], xm)
        early_p = send(wt1.at[b, right], xrp.at[b], xp)
        early_m = send(wt1.at[a, left], xrm.at[a], xm)
        yield
        relay_p.wait_recv()
        for i in range(half):
            wt1[lo + i, right] = add(wt1[lo + i, right], xlp[lo // 2 + i])
        late_p = send(wt1.at[a, right], xrp.at[a], xp)
        relay_m.wait_recv()
        for i in range(half):
            wt1[lo + half + i, left] = add(wt1[lo + half + i, left], xlm[lo // 2 + i])
        late_m = send(wt1.at[b, left], xrm.at[b], xm)
        yield
        for copy in (early_p, early_m, late_p, late_m):
            copy.wait_recv()

        def one(j, carry):
            total = wt1[j, mine].astype(F32) + xrp[j].astype(F32) + xrm[j].astype(F32)
            xr[block_of(j)] = total.astype(BF)
            return carry

        lax.fori_loop(lo, lo + 2 * half, one, 0)
        yield

    def along_z(buf, first, rows, from_m, from_p, out, lanes):
        half = rows // 2
        up, down, both = pl.ds(first, half), pl.ds(first + half, half), pl.ds(first, rows)
        a = send(buf.at[at_z(4), up], from_m.at[3, up], zp)
        b = send(buf.at[at_z(4), down], from_p.at[3, down], zm)
        yield
        for d in (3, 2, 1):
            part_a, part_b = (up, down) if d == 3 else (both, both)
            a.wait_recv()
            here = at_z(d)
            buf[here, part_a] = add(buf[here, part_a], from_m[d, part_a])
            a = send(buf.at[here, both], from_m.at[d - 1, both], zp)
            b.wait_recv()
            here = at_z(-d)
            buf[here, part_b] = add(buf[here, part_b], from_p[d, part_b])
            b = send(buf.at[here, both], from_p.at[d - 1, both], zm)
            yield
        a.wait_recv()
        b.wait_recv()
        total = buf[z, both].astype(F32) + from_m[0, both].astype(F32) + from_p[0, both].astype(F32)
        out[both, lanes] = total.astype(BF)
        yield

    def along_x_last():
        far, right, left, mine = (pl.multiple_of(at_x(d) * PART, PART) for d in (2, 1, -1, 0))
        half = PART // 2
        up, down = pl.ds(0, half), pl.ds(half, half)
        a = send(zr2.at[pl.ds(far, half)], x2p.at[1, up], xp)
        b = send(zr2.at[pl.ds(pl.multiple_of(far + half, half), half)], x2m.at[1, down], xm)
        yield
        a.wait_recv()
        zr2[pl.ds(right, half)] = add(zr2[pl.ds(right, half)], x2p[1, up])
        a = send(zr2.at[pl.ds(right, PART)], x2p.at[0], xp)
        b.wait_recv()
        low = pl.ds(pl.multiple_of(left + half, half), half)
        zr2[low] = add(zr2[low], x2m[1, down])
        b = send(zr2.at[pl.ds(left, PART)], x2m.at[0], xm)
        yield
        a.wait_recv()
        b.wait_recv()
        total = zr2[pl.ds(mine, PART)].astype(F32) + x2p[0].astype(F32) + x2m[0].astype(F32)
        wg[:, LX:] = total.astype(BF)
        yield

    in_w.wait()
    acc[...] = jnp.zeros_like(acc)
    g_sib.wait_recv()
    grads(0, 2, first_group)

    for m in moves:
        m.wait_recv()
    from_prv, from_nxt, from_acr = moved(at_dp(-1), 6), moved(at_dp(1), 7), moved(at_dp(NDP // 2), 5)
    last = jnp.where(from_prv, att_recv[0].astype(F32),
                     jnp.where(from_nxt, att_recv[1].astype(F32),
                               jnp.where(from_acr, att_recv[2].astype(F32), unit(att_home, 5))))
    att[pl.ds(0, 5 * UNIT), :] = att_home[pl.ds(0, 5 * UNIT), :]
    att[pl.ds(5 * UNIT, UNIT), :] = last.astype(BF)

    terms(0, 2, first_group)
    x1 = along_x(0, 1, first_group)
    next(x1)

    def turn(i):
        return lax.rem(y + 2 + 3 * i, NY)

    p_base = len(sent)

    def p_copy(i):
        return pltpu.make_async_remote_copy(
            src_ref=psend.at[i], dst_ref=precv.at[i], send_sem=ss.at[p_base + i],
            recv_sem=rs.at[p_base + i], device_id=sib, device_id_type=MESH)

    sent.extend(p_copy(i) for i in range(NY))

    def for_sibling():
        def one(i, carry):
            psend[i] = nn(att[...], w[:, cols_of(2 * turn(i) + 1 - c)]).astype(BF)
            p_copy(i).start()
            return carry

        lax.fori_loop(0, NY, one, 0)

    def for_me():
        def one(i, carry):
            rbuf[i] = nn(att[...], w[:, cols_of(2 * turn(i) + c)]).astype(BF)
            return carry

        lax.fori_loop(0, NY, one, 0)

    def merge():
        for i in range(NY):
            sent[p_base + i].wait_recv()
            rbuf[i] = add(rbuf[i], precv[i])

    held = {"near": [], "yo": [], "seven": []}

    def beside(arrived, slot, part, into):
        arrived.wait_recv()
        held[into].append(send(gb.at[slot, part], gb.at[slot + (2 if slot < 6 else 1), part], sib))

    def ahead():
        for i in range(2):
            beside(first[i][0], 2, quarters[i], "near")
            beside(first[i][1], 3, quarters[i + 2], "near")

    def pass_on():
        for i in range(2):
            held["yo"].append((send(gb.at[2, quarters[i]], gb.at[6, quarters[i]], yp),
                               send(gb.at[3, quarters[i + 2]], gb.at[6, quarters[i + 2]], ym)))

    def near():
        for i in range(2):
            beside(later[i][0], 2, quarters[i + 2], "near")
            beside(later[i][1], 3, quarters[i], "near")

    def second():
        for copy in held["near"]:
            copy.wait_recv()
        terms(4, 6, second_group)

    def far():
        for i in range(2):
            beside(held["yo"][i][0], 6, quarters[i], "seven")
            beside(held["yo"][i][1], 6, quarters[i + 2], "seven")

    def third():
        for copy in held["seven"]:
            copy.wait_recv()
        terms(7, 8, third_group)

    def y_far():
        held["r_far"] = [send(rbuf.at[0, top], yrp.at[1, top], yp),
                         send(rbuf.at[0, bot], yrm.at[1, bot], ym)]

    def y_early():
        held["r"] = [send(rbuf.at[1, bot], yrp.at[0, bot], yp),
                     send(rbuf.at[3, top], yrm.at[0, top], ym)]

    def y_late():
        held["r_far"][0].wait_recv()
        rbuf[1, top] = add(rbuf[1, top], yrp[1, top])
        held["r"].append(send(rbuf.at[1, top], yrp.at[0, top], yp))
        held["r_far"][1].wait_recv()
        rbuf[3, bot] = add(rbuf[3, bot], yrm[1, bot])
        held["r"].append(send(rbuf.at[3, bot], yrm.at[0, bot], ym))

    def y_end():
        for copy in held["r"]:
            copy.wait_recv()
        mixed[...] = (rbuf[2].astype(F32) + yrp[0].astype(F32) + yrm[0].astype(F32)).astype(BF)
        out_mixed.start()

    def back():
        agw[...] = acc[...].astype(BF)
        tail = agw.at[pl.ds(5 * UNIT, UNIT)]
        held["back"] = [send(tail, back_recv.at[i], to) for i, to in enumerate((prv, nxt, acr))]

    def home():
        for copy in held["back"]:
            copy.wait_recv()
        got = from_prv | from_nxt | from_acr
        ghome[pl.ds(0, 5 * UNIT), :] = agw[pl.ds(0, 5 * UNIT), :]
        for u in (5, 6, 7):
            value = jnp.zeros((UNIT, INN), F32)
            for i, slot in enumerate((6, 7, 5)):
                hit = moved(dp, slot) & (starts[slot] == u * UNIT)
                value = jnp.where(hit, back_recv[i].astype(F32), value)
            if u == 5:
                value = jnp.where(got, value, unit(agw, 5))
            ghome[pl.ds(u * UNIT, UNIT), :] = value.astype(BF)

    def backward(h, carry):
        at = pl.multiple_of(h * HEAD, HEAD)
        q_t = qkv[0, :, pl.ds(at, HEAD)].astype(F32).T.astype(BF)
        g_t = ghome[:, pl.ds(at, HEAD)].astype(F32).T.astype(BF)
        dk_t[...] = jnp.zeros_like(dk_t)
        dv_t[...] = jnp.zeros_like(dv_t)
        for i, (lo, hi) in enumerate(WINDOWS):
            rows, keys = pl.ds(i * 128, 128), pl.ds(lo, hi - lo)
            k = qkv[1, keys, pl.ds(at, HEAD)]
            v = qkv[2, keys, pl.ds(at, HEAD)]
            p = probs[h, rows, keys]
            dp_ = nt(ghome[rows, pl.ds(at, HEAD)], v)
            mean = jnp.sum(p * dp_, axis=-1, keepdims=True)
            ds = (p * (dp_ - mean) * DOWN).astype(BF)
            dqkv[0, rows, pl.ds(at, HEAD)] = nn(ds, k).astype(BF)
            mine = slice(i * 128, (i + 1) * 128)
            dk_t[:, keys] += nn(q_t[:, mine], ds)
            dv_t[:, keys] += nn(g_t[:, mine], p.astype(BF))
        dqkv[1, :, pl.ds(at, HEAD)] = dk_t[...].T.astype(BF)
        dqkv[2, :, pl.ds(at, HEAD)] = dv_t[...].T.astype(BF)
        return carry

    def heads(lo, hi):
        lax.fori_loop(lo, hi, backward, 0)
        if hi == HEADS:
            out_dqkv.start()

    lanes = slice(None)
    x2a = along_x(2, 1, second_group)
    x2b = along_x(4, 1, second_group)
    x3 = along_x(6, 1, third_group)
    z2 = [along_z(wt2, i * ZROWS, ZROWS, z2p, z2m, zr2, lanes) for i in range(COLS // ZROWS)]
    z1 = [along_z(xr, i * XROWS, XROWS, z1p, z1m, wg, pl.ds(0, LX)) for i in range(PART // XROWS)]
    xl = [along_x_last()]

    def go(rings):
        for ring in rings:
            next(ring)

    todo = {
        "P": for_sibling, "Q": for_me, "M": merge, "S": ahead, "F": pass_on, "N": near, "T2A": lambda: terms(2, 4, second_group), "T2B": second, "W": far,
        "T3A": lambda: terms(6, 7, third_group), "T3B": third, "G2": lambda: grads(2, 6, second_group), "G3": lambda: grads(6, 8, third_group),
        "YF": y_far, "YE": y_early, "YL": y_late, "YD": y_end, "BK": back, "HM": home,
        "B0": lambda: heads(0, 1), "B1": lambda: heads(1, 2), "B2": lambda: heads(2, 3),
        "B12": lambda: heads(1, 3), "B": lambda: heads(0, 3),
        "X1": lambda: next(x1), "A": lambda: next(x2a), "C": lambda: next(x2b), "X3": lambda: next(x3),
        "Z2": lambda: go(z2), "Z1": lambda: go(z1), "XL": lambda: go(xl),
    }
    for name in ORDER:
        todo[name]()
    out_wg.start()
    for copy in sent:
        copy.wait_send()
    for copy in (out_mixed, out_dqkv, out_wg):
        copy.wait()


def scratch():
    v = pltpu.VMEM
    return [
        v((3, HOME, INN), BF), v((INN, 8 * COLS), BF), v((8, CAP, COLS), BF), v((HOME, HOME), F32),
        v((HEADS, HOME, HOME), F32), v((HOME, INN), BF), v((3, UNIT, INN), BF), v((3, UNIT, INN), BF),
        v((CAP, INN), BF), v((CAP, INN), F32), v((CAP, INN), BF), v((3, UNIT, INN), BF),
        v((HOME, INN), BF), v((HEAD, HOME), F32), v((HEAD, HOME), F32),
        v((8, COLS, LX), BF), v((8, COLS, LZ), BF),
        v((4, CAP, COLS), BF), v((4, CAP, COLS), BF), v((4, CAP, COLS), BF),
        v((2, CAP, COLS), BF), v((2, CAP, COLS), BF),
        v((4, PART, LX), BF), v((4, PART, LX), BF), v((8, PART, LX), BF), v((8, PART, LX), BF),
        v((8, PART, LX), BF),
        v((4, PART, LX), BF), v((4, PART, LX), BF), v((4, COLS, LZ), BF), v((4, COLS, LZ), BF),
        v((COLS, LZ), BF), v((2, PART, LZ), BF), v((2, PART, LZ), BF),
        v((CAP, COLS), BF), v((3, HOME, INN), BF), v((PART, INN), BF),
        pltpu.SemaphoreType.DMA((112,)), pltpu.SemaphoreType.DMA((112,)), pltpu.SemaphoreType.DMA((6,)),
    ]


def body(qkv_rows, out_weight, out_grad, image_len, dest_rank, dest_offset):
    smem = pl.BlockSpec(memory_space=pltpu.SMEM)
    anywhere = pl.BlockSpec(memory_space=pl.ANY)
    mixed, dqkv, turned = pl.pallas_call(
        kernel,
        out_shape=(
            jax.ShapeDtypeStruct((CAP, COLS), BF),
            jax.ShapeDtypeStruct((3, HOME, INN), BF),
            jax.ShapeDtypeStruct((192, INN), BF),
        ),
        in_specs=[smem, smem, anywhere, anywhere, anywhere],
        out_specs=(anywhere, anywhere, anywhere),
        scratch_shapes=scratch(),
        compiler_params=pltpu.CompilerParams(
            collective_id=0, has_side_effects=True, vmem_limit_bytes=60 * 2**20),
    )(image_len, dest_rank, jnp.transpose(qkv_rows, (1, 0, 2)), out_weight, out_grad)
    return mixed, jnp.transpose(dqkv, (1, 0, 2)), turned.T


def solution(mesh):
    return jax.shard_map(
        body,
        mesh=mesh,
        in_specs=(P("dp", None, "mp"), P("mp", None), P("dp", "mp"), P(), P(), P()),
        out_specs=(P("dp", "mp"), P("dp", None, "mp"), P("mp", "dp")),
        check_vma=False,
    )
```

time: 93 us -> 77 us (0.83)
  Pallas kernels: 84.4 us -> 72.1 us
  local copies, waits for them, and re-layouts: 7.7 us -> 3.7 us
    pallas_call x1, Pallas kernels: 84.4 us -> 72.1 us  [body(): pl.pallas_call(kernel, out_shape=(jax.ShapeDtypeStruct((CAP, COLS), BF),...]
    pallas_call x1 -> x0, local copies, waits for them, and re-layouts: 1.57 us -> none  [body(): pl.pallas_call(kernel, out_shape=(jax.ShapeDtypeStruct((CAP, COLS), BF),...]
    reshape x1 -> x0, local copies, waits for them, and re-layouts: 1.41 us -> none  [body(): qkv_rows.reshape(HOME, 3 * INN)]
    unnamed x8 -> x7, local copies, waits for them, and re-layouts: 4.6 us -> 3.7 us
where the time goes in v2:
time: 77 us; the launch traced here: 76.5 us
  Pallas kernels  72.1 us (94%)
  local copies, waits for them, and re-layouts  3.7 us (5%)
    pallas_call x1, Pallas kernels, body(): pl.pallas_call(kernel, out_shape=(jax.ShapeDtypeStruct((CAP, COLS), BF),...  72.1 us
    unnamed x7, local copies, waits for them, and re-layouts  3.7 us

profile of v2, /device:TPU:24, one launch (start us, length us, event | category | flops | bytes accessed | tf_op | source)
XLA Modules:
  0.0 76.5 jit_solution(14210328727308155682)
XLA Ops:
  0.6 72.1 %shard_map.76 = (bf16[384,768]{1,0:T(8,128)(2,1)}, bf16[3,512,384]{2,1,0:T(8,128)(2,1)}, bf16[192,384]{1,0:T(8,128)(2,1)}) custom-call(s32[256]{0:T(256)} %len_ref.1, s32[256]{0:T(256)} %dest_ref.1, bf16[3,512,384]{2,1,0:T(8,128)(2,1)} %bitcast.4, bf16[384,6144]{1,0:T(8,128)(2,1)} %w_hbm.1, bf16[384,768]{1,0:T(8,128)(2,1)} %g_hbm.1), custom_call_target="tpu_custom_call" | custom-call | tf_op jit(solution)/shard_map/pallas_call | solution.py:482
  72.8 0.0 copy-start
  72.8 2.0 %copy.11 = bf16[384,768]{1,0:T(8,128)(2,1)} copy(bf16[384,768]{1,0:T(8,128)(2,1)} %get-tuple-element.12) | data formatting | bytes 1179648
  74.8 0.0 copy-done
  74.8 0.0 copy-start.1
  74.8 1.0 %copy.12 = bf16[512,3,384]{2,0,1:T(8,128)(2,1)} copy(bf16[512,3,384]{2,0,1:T(8,128)(2,1)S(1)} %bitcast.3) | data formatting | bytes 2359296
  75.8 0.0 copy-done.1
  75.8 0.7 copy.13
Async XLA Ops:
  72.8 2.0 %copy-start = (bf16[3,512,384]{2,1,0:T(8,128)(2,1)S(1)}, bf16[3,512,384]{2,1,0:T(8,128)(2,1)}, u32[]{:S(2)}) copy-start(bf16[3,512,384]{2,1,0:T(8,128)(2,1)} %get-tuple-element.7) | copy-start | bytes 3538948
  74.8 1.0 %copy-start.1 = (bf16[192,384]{1,0:T(8,128)(2,1)S(1)}, bf16[192,384]{1,0:T(8,128)(2,1)}, u32[]{:S(2)}) copy-start(bf16[192,384]{1,0:T(8,128)(2,1)} %get-tuple-element.8) | copy-start | bytes 442372

commit v3 on v2

--- a/solution.py
+++ b/solution.py
@@ -32,9 +32,9 @@
 
 
 ORDER = (
-    "P", "S", "F", "Q", "X1", "N", "T2A", "A", "T2B", "C", "M", "A", "X1", "W", "YF", "YE", "T3A", "T3B",
-    "Z2", "X3", "C", "A", "G2", "Z2", "G3", "BK", "YL", "C", "X3", "Z2", "HM", "B0", "X3", "Z1", "Z2",
-    "B1", "Z1", "Z2", "XL", "Z1", "B2", "XL", "Z1", "XL", "YD", "Z1",
+    "P", "S", "F", "Q", "X1", "N", "T2A", "A", "T2B", "C", "M", "A", "G2", "X1", "W", "YF", "YE", "T3A",
+    "T3B", "Z2", "X3", "C", "A", "G3", "BK", "Z2", "C", "YL", "X3", "HM", "Z2", "X3", "Z1", "B0", "Z2",
+    "Z1", "B1", "Z2", "XL", "Z1", "YD", "XL", "Z1", "XL", "B2", "Z1",
 )
 
 

time: 77 us -> 76.2 us (0.990)
  no operation moved by 1% of the time
where the time goes in v3:
time: 76.2 us; the launch traced here: 76 us
  Pallas kernels  71.7 us (94%)
  local copies, waits for them, and re-layouts  3.7 us (5%)
    pallas_call x1, Pallas kernels, body(): pl.pallas_call(kernel, out_shape=(jax.ShapeDtypeStruct((CAP, COLS), BF),...  71.7 us
    unnamed x7, local copies, waits for them, and re-layouts  3.7 us

profile of v3, /device:TPU:24, one launch (start us, length us, event | category | flops | bytes accessed | tf_op | source)
XLA Modules:
  0.0 76.0 jit_solution(623118817111106831)
XLA Ops:
  0.6 71.7 %shard_map.76 = (bf16[384,768]{1,0:T(8,128)(2,1)}, bf16[3,512,384]{2,1,0:T(8,128)(2,1)}, bf16[192,384]{1,0:T(8,128)(2,1)}) custom-call(s32[256]{0:T(256)} %len_ref.1, s32[256]{0:T(256)} %dest_ref.1, bf16[3,512,384]{2,1,0:T(8,128)(2,1)} %bitcast.4, bf16[384,6144]{1,0:T(8,128)(2,1)} %w_hbm.1, bf16[384,768]{1,0:T(8,128)(2,1)} %g_hbm.1), custom_call_target="tpu_custom_call" | custom-call | tf_op jit(solution)/shard_map/pallas_call | solution.py:482
  72.3 0.0 copy-start
  72.3 2.0 %copy.11 = bf16[384,768]{1,0:T(8,128)(2,1)} copy(bf16[384,768]{1,0:T(8,128)(2,1)} %get-tuple-element.12) | data formatting | bytes 1179648
  74.3 0.0 copy-done
  74.3 0.0 copy-start.1
  74.3 1.0 %copy.12 = bf16[512,3,384]{2,0,1:T(8,128)(2,1)} copy(bf16[512,3,384]{2,0,1:T(8,128)(2,1)S(1)} %bitcast.3) | data formatting | bytes 2359296
  75.3 0.0 copy-done.1
  75.4 0.7 copy.13
Async XLA Ops:
  72.3 2.0 %copy-start = (bf16[3,512,384]{2,1,0:T(8,128)(2,1)S(1)}, bf16[3,512,384]{2,1,0:T(8,128)(2,1)}, u32[]{:S(2)}) copy-start(bf16[3,512,384]{2,1,0:T(8,128)(2,1)} %get-tuple-element.7) | copy-start | bytes 3538948
  74.3 1.0 %copy-start.1 = (bf16[192,384]{1,0:T(8,128)(2,1)S(1)}, bf16[192,384]{1,0:T(8,128)(2,1)}, u32[]{:S(2)}) copy-start(bf16[192,384]{1,0:T(8,128)(2,1)} %get-tuple-element.8) | copy-start | bytes 442372

commit v4 on v3

--- a/solution.py
+++ b/solution.py
@@ -111,6 +111,9 @@
     for i in range(2):
         first[i] = (send(gb.at[0, quarters[i]], gb.at[2, quarters[i]], yp),
                     send(gb.at[0, quarters[i + 2]], gb.at[3, quarters[i + 2]], ym))
+    for i in range(2):
+        later[i] = (send(gb.at[0, quarters[i + 2]], gb.at[2, quarters[i + 2]], yp),
+                    send(gb.at[0, quarters[i]], gb.at[3, quarters[i]], ym))
     g_sib = send(gb.at[0], gb.at[1], sib)
 
     def ends_of(rank):
@@ -152,9 +155,6 @@
         return carry
 
     lax.fori_loop(0, HEADS, forward, 0)
-    for i in range(2):
-        later[i] = (send(gb.at[0, quarters[i + 2]], gb.at[2, quarters[i + 2]], yp),
-                    send(gb.at[0, quarters[i]], gb.at[3, quarters[i]], ym))
 
     def unit(ref, u):
         return ref[pl.ds(u * UNIT, UNIT), :].astype(F32)

time: 76.2 us -> 76.2 us (level)
  no operation moved by 1% of the time
where the time goes in v4:
time: 76.2 us; the launch traced here: 76 us
  Pallas kernels  71.7 us (94%)
  local copies, waits for them, and re-layouts  3.7 us (5%)
    pallas_call x1, Pallas kernels, body(): pl.pallas_call(kernel, out_shape=(jax.ShapeDtypeStruct((CAP, COLS), BF),...  71.7 us
    unnamed x7, local copies, waits for them, and re-layouts  3.7 us

profile of v4, /device:TPU:24, one launch (start us, length us, event | category | flops | bytes accessed | tf_op | source)
XLA Modules:
  0.0 76.0 jit_solution(8538854525434751621)
XLA Ops:
  0.6 71.7 %shard_map.76 = (bf16[384,768]{1,0:T(8,128)(2,1)}, bf16[3,512,384]{2,1,0:T(8,128)(2,1)}, bf16[192,384]{1,0:T(8,128)(2,1)}) custom-call(s32[256]{0:T(256)} %len_ref.1, s32[256]{0:T(256)} %dest_ref.1, bf16[3,512,384]{2,1,0:T(8,128)(2,1)} %bitcast.4, bf16[384,6144]{1,0:T(8,128)(2,1)} %w_hbm.1, bf16[384,768]{1,0:T(8,128)(2,1)} %g_hbm.1), custom_call_target="tpu_custom_call" | custom-call | tf_op jit(solution)/shard_map/pallas_call | solution.py:482
  72.3 0.0 copy-start
  72.3 2.0 %copy.11 = bf16[384,768]{1,0:T(8,128)(2,1)} copy(bf16[384,768]{1,0:T(8,128)(2,1)} %get-tuple-element.12) | data formatting | bytes 1179648
  74.3 0.0 copy-done
  74.4 0.0 copy-start.1
  74.4 1.0 %copy.12 = bf16[512,3,384]{2,0,1:T(8,128)(2,1)} copy(bf16[512,3,384]{2,0,1:T(8,128)(2,1)S(1)} %bitcast.3) | data formatting | bytes 2359296
  75.4 0.0 copy-done.1
  75.4 0.7 copy.13
Async XLA Ops:
  72.3 2.0 %copy-start = (bf16[3,512,384]{2,1,0:T(8,128)(2,1)S(1)}, bf16[3,512,384]{2,1,0:T(8,128)(2,1)}, u32[]{:S(2)}) copy-start(bf16[3,512,384]{2,1,0:T(8,128)(2,1)} %get-tuple-element.7) | copy-start | bytes 3538948
  74.4 1.0 %copy-start.1 = (bf16[192,384]{1,0:T(8,128)(2,1)S(1)}, bf16[192,384]{1,0:T(8,128)(2,1)}, u32[]{:S(2)}) copy-start(bf16[192,384]{1,0:T(8,128)(2,1)} %get-tuple-element.8) | copy-start | bytes 442372
